TPU v7x, 32 devices: a whole 2x2x4 slice. The times are simulated.
32 devices in a mesh: grp: 4 (over z), own: 8 (over y, x, core).
Axes of the slice: x: 2, y: 2, z: 4, core: 2. Of those that a mesh axis runs over, the one named last changes fastest.
Arguments:
- tokens: bfloat16 [16384, 768], P(('grp', 'own')), may hold values from -6 to 6
- doc_ids: int32 [16384], P(('grp', 'own')), may hold values from 0 to 4, as said below
- cotangent: bfloat16 [16384, 768], P(('grp', 'own')), may hold values from -6 to 6
- norm1_gain: bfloat16 [768], P('own'), may hold values from 0.5 to 1.5
- norm1_shift: bfloat16 [768], P('own'), may hold values from -1.75 to 1.75
- qkv_weight: bfloat16 [768, 2304], P('own'), may hold values from -0.21875 to 0.21875
- query_bias: bfloat16 [768], P('own'), may hold values from -3 to 3
- value_bias: bfloat16 [768], P('own'), may hold values from -3 to 3
- out_weight: bfloat16 [768, 768], P('own'), may hold values from -0.625 to 0.625
- out_bias: bfloat16 [768], P('own'), may hold values from -1.75 to 1.75
- norm2_gain: bfloat16 [768], P('own'), may hold values from 0.5 to 1.5
- norm2_shift: bfloat16 [768], P('own'), may hold values from -1.75 to 1.75
- fc_weight: bfloat16 [768, 3072], P('own'), may hold values from -0.21875 to 0.21875
- fc_bias: bfloat16 [3072], P('own'), may hold values from -3 to 3
- proj_weight: bfloat16 [3072, 768], P('own'), may hold values from -0.109375 to 0.109375
- proj_bias: bfloat16 [768], P('own'), may hold values from -1.75 to 1.75
Outputs:
- activations: bfloat16 [16384, 768], P(('grp', 'own'))
- tokens_grad: float32 [16384, 768], P(('grp', 'own'))
- norm1_gain_grad: float32 [768], P('own')
- norm1_shift_grad: float32 [768], P('own')
- qkv_weight_grad: float32 [768, 2304], P('own')
- query_bias_grad: float32 [768], P('own')
- value_bias_grad: float32 [768], P('own')
- out_weight_grad: float32 [768, 768], P('own')
- out_bias_grad: float32 [768], P('own')
- norm2_gain_grad: float32 [768], P('own')
- norm2_shift_grad: float32 [768], P('own')
- fc_weight_grad: float32 [768, 3072], P('own')
- fc_bias_grad: float32 [3072], P('own')
- proj_weight_grad: float32 [3072, 768], P('own')
- proj_bias_grad: float32 [768], P('own')
Inputs may be any that keep to these rules, and one draw needn't show every extreme that they name: `doc_ids`: each row of 512 tokens numbers its documents 1, 2, ... in order from its first token, then may end with padding numbered 0.
All inputs are finite; a program needn't handle non-finite values.
Results may differ from a plain program's by a relative error of at most 0.017.
Values may be sent and summed in bfloat16 or wider, within the bound.
A program may use at most 192 MiB of HBM per device.

v0:
```python
import jax
import jax.numpy as jnp
from jax import lax
from jax.sharding import PartitionSpec as P

HEADS = 12
HEAD_DIM = 64
USES = 2


EPSILON = 1e-05


def as_sent(shard):
    return jax.tree.map(lambda a: a.astype(jnp.bfloat16) if a.dtype == jnp.float32 else a, shard)


def normalize(x, gain, shift):
    centre = x - jnp.mean(x, axis=-1, keepdims=True)
    spread = jnp.mean(centre * centre, axis=-1, keepdims=True)
    return centre * lax.rsqrt(spread + EPSILON) * gain + shift


def smooth(inner):
    return jax.nn.gelu(inner, approximate=True)


def visible(doc):
    count = doc.shape[0]
    row = lax.broadcasted_iota(jnp.int32, (count, count), 0)
    col = lax.broadcasted_iota(jnp.int32, (count, count), 1)
    same = doc[:, None] == doc[None, :]
    return same & (col <= row) & ((doc[None, :] != 0) | (row == col))


def forward_layer(x, weights, mask):
    (
        gain_one,
        shift_one,
        w_qkv,
        bias_query,
        bias_value,
        w_out,
        bias_out,
        gain_two,
        shift_two,
        w_fc,
        bias_fc,
        w_proj,
        bias_proj,
    ) = weights
    width = w_qkv.shape[0]
    count = x.shape[0]
    scale = HEAD_DIM ** (-0.5)
    f32 = jnp.float32
    h_one = normalize(x, gain_one.astype(f32), shift_one.astype(f32)).astype(jnp.bfloat16)
    qkv_bias = jnp.concatenate(
        [bias_query.astype(f32), jnp.zeros((width,), f32), bias_value.astype(f32)]
    )
    packed = (jnp.dot(h_one, w_qkv, preferred_element_type=f32) + qkv_bias).astype(jnp.bfloat16)
    query = packed[:, :width].reshape(count, HEADS, HEAD_DIM)
    key = packed[:, width : 2 * width].reshape(count, HEADS, HEAD_DIM)
    value = packed[:, 2 * width :].reshape(count, HEADS, HEAD_DIM)
    scores = jnp.einsum("thd,shd->hts", query, key, preferred_element_type=f32) * scale
    scores = jnp.where(mask[None], scores, -1e30)
    probs = jax.nn.softmax(scores, axis=-1)
    probs_low = probs.astype(jnp.bfloat16)
    mixed = jnp.einsum("hts,shd->thd", probs_low, value, preferred_element_type=f32)
    mixed = mixed.reshape(count, width).astype(jnp.bfloat16)
    middle = x + (jnp.dot(mixed, w_out, preferred_element_type=f32) + bias_out.astype(f32))
    h_two = normalize(middle, gain_two.astype(f32), shift_two.astype(f32)).astype(jnp.bfloat16)
    inner = jnp.dot(h_two, w_fc, preferred_element_type=f32) + bias_fc.astype(f32)
    active = smooth(inner).astype(jnp.bfloat16)
    result = middle + (jnp.dot(active, w_proj, preferred_element_type=f32) + bias_proj.astype(f32))
    kept = (h_one, query, key, value, probs, probs_low, mixed, middle, h_two, inner, active)
    return (result, kept)


def backward_layer(x, weights, mask, grad):
    (
        gain_one,
        shift_one,
        w_qkv,
        bias_query,
        bias_value,
        w_out,
        bias_out,
        gain_two,
        shift_two,
        w_fc,
        bias_fc,
        w_proj,
        bias_proj,
    ) = weights
    result, kept = forward_layer(x, weights, mask)
    h_one, query, key, value, probs, probs_low, mixed, middle, h_two, inner, active = kept
    width = w_qkv.shape[0]
    count = x.shape[0]
    scale = HEAD_DIM ** (-0.5)
    f32 = jnp.float32
    grad_branch = grad.astype(jnp.bfloat16)
    g_wproj = jnp.einsum("tf,td->fd", active, grad_branch, preferred_element_type=f32)
    g_bproj = jnp.sum(grad_branch.astype(f32), axis=0)
    d_active = jnp.einsum("td,fd->tf", grad_branch, w_proj, preferred_element_type=f32)
    unused, pull_smooth = jax.vjp(smooth, inner)
    d_inner = pull_smooth(d_active)[0].astype(jnp.bfloat16)
    g_wfc = jnp.einsum("td,tf->df", h_two, d_inner, preferred_element_type=f32)
    g_bfc = jnp.sum(d_inner.astype(f32), axis=0)
    d_htwo = jnp.einsum("tf,df->td", d_inner, w_fc, preferred_element_type=f32)
    unused, pull_two = jax.vjp(normalize, middle, gain_two.astype(f32), shift_two.astype(f32))
    d_mid, g_gain2, g_shift2 = pull_two(d_htwo)
    d_middle = grad + d_mid
    d_attn = d_middle.astype(jnp.bfloat16)
    g_wout = jnp.einsum("td,te->de", mixed, d_attn, preferred_element_type=f32)
    g_bout = jnp.sum(d_attn.astype(f32), axis=0)
    d_mixed = jnp.einsum("te,de->td", d_attn, w_out, preferred_element_type=f32).astype(
        jnp.bfloat16
    )
    d_mixed = d_mixed.reshape(count, HEADS, HEAD_DIM)
    d_probs = jnp.einsum("thd,shd->hts", d_mixed, value, preferred_element_type=f32)
    d_value = jnp.einsum("hts,thd->shd", probs_low, d_mixed, preferred_element_type=f32)
    d_scores = probs * (d_probs - jnp.sum(d_probs * probs, axis=-1, keepdims=True))
    d_scores = d_scores.astype(jnp.bfloat16)
    d_query = jnp.einsum("hts,shd->thd", d_scores, key, preferred_element_type=f32) * scale
    d_key = jnp.einsum("hts,thd->shd", d_scores, query, preferred_element_type=f32) * scale
    d_packed = jnp.concatenate(
        [d_query.reshape(count, width), d_key.reshape(count, width), d_value.reshape(count, width)],
        axis=1,
    ).astype(jnp.bfloat16)
    g_wqkv = jnp.einsum("td,te->de", h_one, d_packed, preferred_element_type=f32)
    column_sums = jnp.sum(d_packed.astype(f32), axis=0)
    g_bquery = column_sums[:width]
    g_bvalue = column_sums[2 * width :]
    d_hone = jnp.einsum("te,de->td", d_packed, w_qkv, preferred_element_type=f32)
    unused, pull_one = jax.vjp(normalize, x, gain_one.astype(f32), shift_one.astype(f32))
    d_input, g_gain1, g_shift1 = pull_one(d_hone)
    terms = (
        g_gain1,
        g_shift1,
        g_wqkv,
        g_bquery,
        g_bvalue,
        g_wout,
        g_bout,
        g_gain2,
        g_shift2,
        g_wfc,
        g_bfc,
        g_wproj,
        g_bproj,
    )
    return (d_middle + d_input, terms)


def body(
    tokens,
    doc_ids,
    cotangent,
    norm1_gain,
    norm1_shift,
    qkv_weight,
    query_bias,
    value_bias,
    out_weight,
    out_bias,
    norm2_gain,
    norm2_shift,
    fc_weight,
    fc_bias,
    proj_weight,
    proj_bias,
):
    shards = (
        norm1_gain,
        norm1_shift,
        qkv_weight,
        query_bias,
        value_bias,
        out_weight,
        out_bias,
        norm2_gain,
        norm2_shift,
        fc_weight,
        fc_bias,
        proj_weight,
        proj_bias,
    )
    mask = visible(doc_ids)

    def fetch():
        return (
            lax.all_gather(shards[0], "own", axis=0, tiled=True),
            lax.all_gather(shards[1], "own", axis=0, tiled=True),
            lax.all_gather(shards[2], "own", axis=0, tiled=True),
            lax.all_gather(shards[3], "own", axis=0, tiled=True),
            lax.all_gather(shards[4], "own", axis=0, tiled=True),
            lax.all_gather(shards[5], "own", axis=0, tiled=True),
            lax.all_gather(shards[6], "own", axis=0, tiled=True),
            lax.all_gather(shards[7], "own", axis=0, tiled=True),
            lax.all_gather(shards[8], "own", axis=0, tiled=True),
            lax.all_gather(shards[9], "own", axis=0, tiled=True),
            lax.all_gather(shards[10], "own", axis=0, tiled=True),
            lax.all_gather(shards[11], "own", axis=0, tiled=True),
            lax.all_gather(shards[12], "own", axis=0, tiled=True),
        )

    current = tokens.astype(jnp.float32)
    saved = []
    for use in range(USES):
        saved.append(current)
        current, kept = forward_layer(current, fetch(), mask)
    grad = cotangent.astype(jnp.float32)
    summed = None
    for use in reversed(range(USES)):
        grad, terms = backward_layer(saved[use], fetch(), mask, grad)
        if summed is None:
            summed = terms
        else:
            summed = tuple((first + second for first, second in zip(summed, terms)))
    owned = (
        lax.psum_scatter(summed[0], "own", scatter_dimension=0, tiled=True),
        lax.psum_scatter(summed[1], "own", scatter_dimension=0, tiled=True),
        lax.psum_scatter(summed[2], "own", scatter_dimension=0, tiled=True),
        lax.psum_scatter(summed[3], "own", scatter_dimension=0, tiled=True),
        lax.psum_scatter(summed[4], "own", scatter_dimension=0, tiled=True),
        lax.psum_scatter(summed[5], "own", scatter_dimension=0, tiled=True),
        lax.psum_scatter(summed[6], "own", scatter_dimension=0, tiled=True),
        lax.psum_scatter(summed[7], "own", scatter_dimension=0, tiled=True),
        lax.psum_scatter(summed[8], "own", scatter_dimension=0, tiled=True),
        lax.psum_scatter(summed[9], "own", scatter_dimension=0, tiled=True),
        lax.psum_scatter(summed[10], "own", scatter_dimension=0, tiled=True),
        lax.psum_scatter(summed[11], "own", scatter_dimension=0, tiled=True),
        lax.psum_scatter(summed[12], "own", scatter_dimension=0, tiled=True),
    )
    final = jax.tree.map(lambda part: part.astype(jnp.float32), lax.psum(as_sent(owned), "grp"))
    return (current.astype(jnp.bfloat16), grad) + tuple(final)


def solution(mesh):
    return jax.shard_map(
        body,
        mesh=mesh,
        in_specs=(
            P(("grp", "own"), None),
            P(("grp", "own")),
            P(("grp", "own"), None),
            P("own"),
            P("own"),
            P("own", None),
            P("own"),
            P("own"),
            P("own", None),
            P("own"),
            P("own"),
            P("own"),
            P("own", None),
            P("own"),
            P("own", None),
            P("own"),
        ),
        out_specs=(
            P(("grp", "own"), None),
            P(("grp", "own"), None),
            P("own"),
            P("own"),
            P("own", None),
            P("own"),
            P("own"),
            P("own", None),
            P("own"),
            P("own"),
            P("own"),
            P("own", None),
            P("own"),
            P("own", None),
            P("own"),
        ),
        check_vma=False,
    )
```

profile of v0, /device:TPU:0, one launch (start us, length us, event | category | flops | bytes accessed | tf_op | source)
XLA Modules:
  0.0 624.9 jit_solution(13215704302195290713)
XLA Ops:
  10.0 1.3 fusion.98
  18.7 26.0 %all-reduce.18 = (bf16[768]{0:T(1024)(128)(2,1)S(1)}, bf16[768]{0:T(1024)(128)(2,1)S(1)}, bf16[768]{0:T(1024)(128)(2,1)S(1)}, bf16[768]{0:T(1024)(128)(2,1)S(1)}...) all-reduce(bf16[768]{0:T(1024)(128)(2,1)S(1)} %dynamic-update-slice, ...), channel_id=1, replica_groups=mesh['grp'=4,'own'=8] {'own'}, use_global_device_ids=true, to_apply=%add.3 | all-reduce | flops 6144 | bytes 24576
  45.5 8.4 %all-gather = bf16[8,1,384]{2,1,0:T(2,128)(2,1)S(1)} all-gather(bf16[1,1,384]{2,1,0:T(2,128)(2,1)S(1)} %reshape.318), channel_id=1, replica_groups=mesh['grp'=4,'own'=8] {'own'}, dimensions={0}, use_global_device_ids=true | all-gather | bytes 6912 | tf_op jit(solution)/shard_map/all_gather | solution.py:202
  54.0 1.3 convert_reduce_fusion.4
  56.3 4.2 fusion.24
  60.6 1.2 copy.72
  62.1 1.2 copy.71
  63.3 10.3 %fusion.99 = (f32[12,512]{1,0:T(8,128)S(1)}, f32[12,512,512]{1,2,0:T(8,128)}) fusion(pred[512,512]{0,1:T(8,128)(4,1)S(1)} %fusion.62, bf16[512,12,64]{0,2,1:T(8,128)(2,1)} %bitcast.112, bf16[512,12,64]{0,2,1:T(8,128)(2,1)S(1)} %bitcast.99), kind=kOutput, calls=%fused_computation.177 | convolution fusion | flops 415236608 | bytes 14442496 | tf_op jit(solution)/shard_map/sub | solution.py:66
  73.6 5.8 fusion.45
  79.4 2.5 fusion.100
  82.2 31.4 %all-gather.10.cloned.1.call-done = bf16[768,3072]{1,0:T(8,128)(2,1)} async-done(((bf16[96,3072]{1,0:T(8,128)(2,1)}), bf16[768,3072]{1,0:T(8,128)(2,1)}) %all-gather.10.cloned.1.call-update) | async-done | bytes 4718608 | tf_op jit(solution)/shard_map/all_gather | solution.py:201
  113.7 7.2 %fusion.85 = f32[512,3072]{1,0:T(8,128)} fusion(bf16[768,3072]{1,0:T(8,128)(2,1)} %all-gather.10.cloned.1.call-done, f32[512,768]{1,0:T(8,128)S(1)} %get-tuple-element.86, f32[768]{0:T(1024)S(1)} %convert_element_type.268, f32[768]{0:T(1024)S(1)} %convert_element_type.267, f32[512]{0:T(512)S(1)} %fusion.67, f32[512]{0:T(512)S(1)} %broadcast_multiply_fusion.2), kind=kOutput, calls=%fused_computation.166 | convolution fusion | flops 2417885184 | bytes 12593152 | tf_op jit(solution)/shard_map/dot_general | solution.py:72
  120.8 33.5 %all-gather.12.cloned.1.call-done = bf16[3072,768]{1,0:T(8,128)(2,1)} async-done(((bf16[384,768]{1,0:T(8,128)(2,1)}), bf16[3072,768]{1,0:T(8,128)(2,1)}) %all-gather.12.cloned.1.call-update) | async-done | bytes 4718608 | tf_op jit(solution)/shard_map/all_gather | solution.py:203
  154.4 7.7 %fusion.101 = (f32[512]{0:T(512)S(1)}, f32[512,768]{1,0:T(8,128)S(1)}) fusion(f32[512,768]{1,0:T(8,128)S(1)} %get-tuple-element.86, f32[768]{0:T(1024)S(1)} %convert_element_type.272, bf16[3072,768]{1,0:T(8,128)(2,1)} %all-gather.12.cloned.1.call-done, f32[512,3072]{1,0:T(8,128)} %fusion.85, f32[3072]{0:T(1024)S(1)} %bitcast.131), kind=kOutput, calls=%fused_computation.179 | convolution fusion | flops 2432826880 | bytes 14173184 | tf_op jit(solution)/shard_map/dot_general | solution.py:74
  162.4 2.1 fusion.25
  166.8 1.4 copy.77
  168.2 1.2 copy.75
  169.3 10.3 %fusion.102 = (f32[12,512]{1,0:T(8,128)S(1)}, f32[12,512,512]{1,2,0:T(8,128)}) fusion(pred[512,512]{0,1:T(8,128)(4,1)S(1)} %fusion.62, bf16[512,12,64]{0,2,1:T(8,128)(2,1)} %bitcast.114, bf16[512,12,64]{0,2,1:T(8,128)(2,1)S(1)} %bitcast.104), kind=kOutput, calls=%fused_computation.180 | convolution fusion | flops 415236608 | bytes 14442496 | tf_op jit(solution)/shard_map/sub | solution.py:66
  179.7 5.9 fusion.51
  187.0 5.1 fusion.87
  192.2 7.3 %convert_reduce_fusion.1 = (f32[3072]{0:T(1024)}, bf16[512,3072]{1,0:T(8,128)(2,1)S(1)}) fusion(f32[512,3072]{1,0:T(8,128)S(1)} %fusion.87, f32[3072]{0:T(1024)S(1)} %bitcast.132, bf16[512,768]{1,0:T(8,128)(2,1)S(1)} %copy-done.24, bf16[3072,768]{1,0:T(8,128)(2,1)S(1)} %bitcast.138), kind=kOutput, calls=%fused_computation.31 | convolution fusion | flops 2452091904 | bytes 14966784 | tf_op jit(solution)/shard_map/td,fd->tf/dot_general | solution.py:104
  199.5 3.5 multiply_reduce_fusion.3
  206.7 1.8 convolution_convert_fusion.1
  208.5 2.3 copy.79
  210.8 10.4 %multiply_reduce_fusion.1 = (f32[12,512]{1,0:T(8,128)S(1)}, f32[12,512,512]{1,2,0:T(8,128)}) fusion(f32[12,512,512]{1,2,0:T(8,128)} %get-tuple-element.90, f32[12,512]{1,0:T(8,128)S(1)} %get-tuple-element.89, bf16[512,12,64]{0,2,1:T(8,128)(2,1)} %bitcast.127, bf16[512,12,64]{0,2,1:T(8,128)(2,1)S(1)} %bitcast.124), kind=kOutput, calls=%fused_computation.5 | convolution fusion | flops 412084224 | bytes 26787840 | tf_op jit(solution)/shard_map/thd,shd->hts/dot_general | solution.py:120
  221.2 1.2 slice-done.4
  222.5 1.2 slice-done.5
  223.6 7.1 %multiply_convert_fusion.1 = bf16[12,512,512]{1,2,0:T(8,128)(2,1)S(1)} fusion(f32[12,512,512]{1,2,0:T(8,128)} %get-tuple-element.95, f32[12,512]{1,0:T(8,128)S(1)} %get-tuple-element.94, f32[12,512,512]{1,2,0:T(8,128)S(1)} %bitcast.92, f32[12,512]{1,0:T(8,128)S(1)} %get-tuple-element.89), kind=kLoop, calls=%fused_computation.4 | loop fusion | flops 12582912 | bytes 31506432 | tf_op jit(solution)/shard_map/convert_element_type | solution.py:123
  232.0 2.0 multiply_convert_fusion.6
  234.0 2.0 fusion.54
  237.8 4.9 multiply_reduce_fusion.4
  244.9 6.6 %convert_reduce_fusion = (f32[3072]{0:T(1024)S(1)}, bf16[512,3072]{1,0:T(8,128)(2,1)S(1)}) fusion(f32[512,3072]{1,0:T(8,128)S(1)} %bitcast.146, f32[3072]{0:T(1024)S(1)} %bitcast.133, bf16[3072,768]{1,0:T(8,128)(2,1)S(1)} %bitcast.140, f32[512,768]{1,0:T(8,128)S(1)} %get-tuple-element.59), kind=kOutput, calls=%fused_computation.30 | convolution fusion | flops 2452485120 | bytes 15753216 | tf_op jit(solution)/shard_map/td,fd->tf/dot_general | solution.py:104
  251.5 3.0 multiply_reduce_fusion.2
  256.9 2.2 convolution_add_fusion.5
  259.1 3.0 convolution_convert_fusion
  262.2 1.4 copy.83
  263.6 11.0 %multiply_reduce_fusion = (f32[12,512]{1,0:T(8,128)S(1)}, f32[12,512,512]{1,2,0:T(8,128)}) fusion(f32[12,512,512]{1,2,0:T(8,128)} %get-tuple-element.84, f32[12,512]{1,0:T(8,128)S(1)} %get-tuple-element.83, bf16[512,12,64]{0,2,1:T(8,128)(2,1)S(1)} %bitcast.125, bf16[512,12,64]{0,2,1:T(8,128)(2,1)S(1)} %bitcast.122), kind=kOutput, calls=%fused_computation.3 | convolution fusion | flops 412084224 | bytes 26787840 | tf_op jit(solution)/shard_map/thd,shd->hts/dot_general | solution.py:120
  274.6 1.4 slice-done.1
  276.0 1.2 slice-done.2
  277.2 6.8 %multiply_convert_fusion = bf16[12,512,512]{1,2,0:T(8,128)(2,1)S(1)} fusion(f32[12,512,512]{1,2,0:T(8,128)} %get-tuple-element.99, f32[12,512]{1,0:T(8,128)S(1)} %get-tuple-element.98, f32[12,512,512]{1,2,0:T(8,128)S(1)} %bitcast.90, f32[12,512]{1,0:T(8,128)S(1)} %get-tuple-element.83), kind=kLoop, calls=%fused_computation.2 | loop fusion | flops 12582912 | bytes 31506432 | tf_op jit(solution)/shard_map/convert_element_type | solution.py:123
  285.3 2.0 multiply_convert_fusion.4
  287.3 2.3 fusion.82
  289.7 3.3 fusion.48
  293.8 5.3 convolution_add_fusion
  299.2 6.5 %fusion.88 = f32[3072,768]{1,0:T(8,128)S(1)} fusion(bf16[512,768]{1,0:T(8,128)(2,1)} %param.18, f32[512,3072]{1,0:T(8,128)} %copy-done.71, f32[3072]{0:T(1024)S(1)} %bitcast.134), kind=kOutput, calls=%fused_computation.169 | convolution fusion | flops 2431647744 | bytes 16527360 | tf_op jit(solution)/shard_map/tf,td->fd/dot_general | solution.py:102
  305.7 11.6 %convolution_add_fusion.1 = f32[3072,768]{1,0:T(8,128)} fusion(f32[3072,768]{1,0:T(8,128)S(1)} %fusion.88, f32[512,768]{1,0:T(8,128)S(1)} %copy-done.3, f32[512,3072]{1,0:T(8,128)} %fusion.85, f32[3072]{0:T(1024)S(1)} %bitcast.135), kind=kOutput, calls=%fused_computation.43 | convolution fusion | flops 2434400256 | bytes 26750976 | tf_op jit(solution)/shard_map/tf,td->fd/dot_general | solution.py:102
  318.0 6.0 fusion.86
  324.0 5.9 convolution_add_fusion.2
  331.7 4.7 fusion.89
  338.4 1.4 convert_reduce_fusion.2
  339.9 1.6 convert_element_type.304
  341.5 29.5 %reduce-scatter.5.cloned.1.call-done = f32[96,2304]{1,0:T(8,128)} async-done(((f32[768,2304]{1,0:T(8,128)}), f32[96,2304]{1,0:T(8,128)}) %reduce-scatter.5.cloned.1.call-update) | async-done | bytes 884752 | tf_op jit(solution)/shard_map/reduce_scatter | solution.py:223
  371.0 2.0 convert_element_type.296
  373.0 78.0 %reduce-scatter.11.cloned.1.call-done = f32[384,768]{1,0:T(8,128)} async-done(((f32[3072,768]{1,0:T(8,128)}), f32[384,768]{1,0:T(8,128)}) %reduce-scatter.11.cloned.1.call-update) | async-done | bytes 1179664 | tf_op jit(solution)/shard_map/reduce_scatter | solution.py:232
  451.0 2.1 convert_element_type.320
  453.2 77.9 %reduce-scatter.9.cloned.1.call-done = f32[96,3072]{1,0:T(8,128)} async-done(((f32[768,3072]{1,0:T(8,128)}), f32[96,3072]{1,0:T(8,128)}) %reduce-scatter.9.cloned.1.call-update) | async-done | bytes 1179664 | tf_op jit(solution)/shard_map/reduce_scatter | solution.py:230
  531.0 2.2 convert_element_type.314
  533.3 24.4 %all-reduce.17 = (bf16[768]{0:T(1024)(128)(2,1)S(1)}, bf16[768]{0:T(1024)(128)(2,1)S(1)}, bf16[768]{0:T(1024)(128)(2,1)S(1)}, bf16[768]{0:T(1024)(128)(2,1)S(1)}...) all-reduce(f32[768]{0:T(1024)S(1)} %add.345, ...), channel_id=2, replica_groups=mesh['grp'=4,'own'=8] {'own'}, use_global_device_ids=true, to_apply=%region_24.25.clone | all-reduce | flops 9216 | bytes 55296
  558.4 13.1 %all-reduce.19 = (bf16[96]{0:T(256)(128)(2,1)S(1)}, bf16[96]{0:T(256)(128)(2,1)S(1)}, bf16[96]{0:T(256)(128)(2,1)S(1)}, bf16[96]{0:T(256)(128)(2,1)S(1)}, bf16[9...) all-reduce(bf16[96]{0:T(256)(128)(2,1)S(1)} %dynamic-slice.43, ...), channel_id=1, replica_groups=mesh['grp'=4,'own'=8] {'grp'}, use_global_device_ids=true, to_apply=%region_25.26 | all-reduce | flops 1152 | bytes 4608 | tf_op jit(solution)/shard_map/psum | solution.py:235
  576.3 3.8 add_add_fusion.4
  580.1 9.1 %add_convert_fusion = bf16[512,768]{1,0:T(8,128)(2,1)} fusion(f32[512,768]{1,0:T(8,128)S(1)} %copy-done.16, bf16[3072,768]{1,0:T(8,128)(2,1)} %all-gather.12.cloned.1.call-done, f32[768]{0:T(1024)S(1)} %copy-done.68, f32[512,3072]{1,0:T(8,128)} %copy-done.71, f32[3072]{0:T(1024)S(1)} %bitcast.136), kind=kOutput, calls=%fused_computation.98 | convolution fusion | flops 2432827392 | bytes 13384704 | tf_op jit(solution)/shard_map/dot_general | solution.py:74
  589.2 22.8 %all-reduce.23.cloned.1.call-done = (bf16[96,2304]{1,0:T(8,128)(2,1)}, bf16[96,768]{1,0:T(8,128)(2,1)}, bf16[96,3072]{1,0:T(8,128)(2,1)}, bf16[384,768]{1,0:T(8,128)(2,1)}) async-done(((bf16[96,2304]{1,0:T(8,128)(2,1)}, bf16[96,768]{1,0:T(8,128)(2,1)}, bf16[96,3072]{1,0:T(8,128)(2,1)}, bf16[384,768]{1,0:T(8,128)(2,1)}), (bf16[96,2304]{1,0:T(8,128)(2,1)}, bf16[96,768]{1,0:T(8,128)(2,1)}, ...) | async-done | bytes 1769488 | tf_op jit(solution)/shard_map/psum | solution.py:235
  612.0 2.2 convert_element_type.315
  614.3 2.2 convert_element_type.321
  (295 shorter events, 38.8 us)
Async XLA Ops:
  7.2 48.2 %copy-start = (bf16[512,768]{1,0:T(8,128)(2,1)S(1)}, bf16[512,768]{1,0:T(8,128)(2,1)}, u32[]{:S(2)}) copy-start(bf16[512,768]{1,0:T(8,128)(2,1)} %param.16) | copy-start | bytes 2359300
  7.2 48.5 %copy-start.56 = (s32[512]{0:T(512)S(1)}, s32[512]{0:T(512)}, u32[]{:S(2)}) copy-start(s32[512]{0:T(512)} %param.17) | copy-start | bytes 6148
  7.2 48.9 %all-gather.6.cloned.1.call-start = ((), (), s32[]{:S(2)}) async-start(), calls=%async_computation.4 | async-start | bytes 3981312 | tf_op jit(solution)/shard_map/all_gather | solution.py:194
  7.9 71.5 %all-gather.8.cloned.1.call-start = ((), (), s32[]{:S(2)}) async-start(), calls=%async_computation.5 | async-start | bytes 1327104 | tf_op jit(solution)/shard_map/all_gather | solution.py:197
  8.7 105.0 %all-gather.10.cloned.1.call-start = ((), (), s32[]{:S(2)}) async-start(), calls=%async_computation.6 | async-start | bytes 5308416 | tf_op jit(solution)/shard_map/all_gather | solution.py:201
  9.4 144.9 %all-gather.12.cloned.1.call-start = ((), (), s32[]{:S(2)}) async-start(), calls=%async_computation.7 | async-start | bytes 5308416 | tf_op jit(solution)/shard_map/all_gather | solution.py:203
  10.0 329.9 %reduce-scatter.7.cloned.1.call-start = ((), (), s32[]{:S(2)}) async-start(), calls=%async_computation.9 | async-start | bytes 2654208 | tf_op jit(solution)/shard_map/reduce_scatter | solution.py:226
  44.8 142.1 %copy-start.50 = (f32[768]{0:T(1024)}, f32[768]{0:T(1024)S(1)}, u32[]{:S(2)}) copy-start(f32[768]{0:T(1024)S(1)} %convert_element_type.268) | copy-start | bytes 9220
  44.8 109.5 %copy-start.67 = (f32[768]{0:T(1024)}, f32[768]{0:T(1024)S(1)}, u32[]{:S(2)}) copy-start(f32[768]{0:T(1024)S(1)} %convert_element_type.272) | copy-start | bytes 9220
  62.1 11.5 %copy-start.10 = (bf16[512,768]{0,1:T(8,128)(2,1)}, bf16[512,768]{0,1:T(8,128)(2,1)S(1)}, u32[]{:S(2)}) copy-start(bf16[512,768]{0,1:T(8,128)(2,1)S(1)} %copy.73) | copy-start | bytes 2359300
  63.2 10.3 %copy-start.40 = (bf16[512,768]{0,1:T(8,128)(2,1)S(1)}, bf16[512,768]{0,1:T(8,128)(2,1)}, u32[]{:S(2)}) copy-start(bf16[512,768]{0,1:T(8,128)(2,1)} %copy.71) | copy-start | bytes 2359300
  154.4 8.0 %copy-start.69 = (bf16[768,2304]{1,0:T(8,128)(2,1)S(1)}, bf16[768,2304]{1,0:T(8,128)(2,1)}, u32[]{:S(2)}) copy-start(bf16[768,2304]{1,0:T(8,128)(2,1)} %all-gather.6.cloned.1.call-done) | copy-start | bytes 10616836
  169.3 10.3 %copy-start.42 = (bf16[512,768]{0,1:T(8,128)(2,1)S(1)}, bf16[512,768]{0,1:T(8,128)(2,1)}, u32[]{:S(2)}) copy-start(bf16[512,768]{0,1:T(8,128)(2,1)} %copy.75) | copy-start | bytes 2359300
  179.7 6.0 copy-start.19
  179.7 6.0 copy-start.70
  186.6 16.5 %copy-start.15 = (f32[512,768]{1,0:T(8,128)}, f32[512,768]{1,0:T(8,128)S(1)}, u32[]{:S(2)}) copy-start(f32[512,768]{1,0:T(8,128)S(1)} %get-tuple-element.92) | copy-start | bytes 4718596
  186.6 16.5 %copy-start.57 = (f32[512]{0:T(512)}, f32[512]{0:T(512)S(1)}, u32[]{:S(2)}) copy-start(f32[512]{0:T(512)S(1)} %broadcast_multiply_fusion) | copy-start | bytes 6148
  186.6 5.5 slice-start.6
  186.9 16.1 %copy-start.63 = (f32[512]{0:T(512)}, f32[512]{0:T(512)S(1)}, u32[]{:S(2)}) copy-start(f32[512]{0:T(512)S(1)} %fusion.69) | copy-start | bytes 6148
  186.9 5.2 copy-start.24
  186.9 5.2 slice-start.7
  187.0 12.5 %slice-start.10 = ((s8[4718592]{0:T(1024)(128)(4,1)}), s8[4194304]{0:T(1024)(128)(4,1)S(1)}, s32[]{:S(2)}) async-start(s8[4718592]{0:T(1024)(128)(4,1)} %bitcast.141), calls=%async_computation.23 | async-start | bytes 8388608
  192.1 7.4 %copy-start.71 = (f32[512,3072]{1,0:T(8,128)}, f32[512,3072]{1,0:T(8,128)S(1)}, u32[]{:S(2)}) copy-start(f32[512,3072]{1,0:T(8,128)S(1)} %fusion.87) | copy-start | bytes 18874372
  192.1 7.4 %slice-start.11 = ((s8[4718592]{0:T(1024)(128)(4,1)}), s8[524288]{0:T(1024)(128)(4,1)S(1)}, s32[]{:S(2)}) async-start(s8[4718592]{0:T(1024)(128)(4,1)} %bitcast.141), calls=%async_computation.24 | async-start | bytes 1048576
  205.8 5.0 copy-start.43
  210.8 10.4 %slice-start.3 = ((s8[12582912]{0:T(1024)(128)(4,1)}), s8[4194304]{0:T(1024)(128)(4,1)S(1)}, s32[]{:S(2)}) async-start(s8[12582912]{0:T(1024)(128)(4,1)} %bitcast.91), calls=%async_computation.16 | async-start | bytes 8388608
  210.8 11.6 %slice-start.4 = ((s8[12582912]{0:T(1024)(128)(4,1)}), s8[4194304]{0:T(1024)(128)(4,1)S(1)}, s32[]{:S(2)}) async-start(s8[12582912]{0:T(1024)(128)(4,1)} %bitcast.91), calls=%async_computation.17 | async-start | bytes 8388608
  210.8 12.8 %slice-start.5 = ((s8[12582912]{0:T(1024)(128)(4,1)}), s8[4194304]{0:T(1024)(128)(4,1)S(1)}, s32[]{:S(2)}) async-start(s8[12582912]{0:T(1024)(128)(4,1)} %bitcast.91), calls=%async_computation.18 | async-start | bytes 8388608
  231.9 5.0 copy-start.12
  236.1 6.7 %copy-start.35 = (bf16[12,64,512]{2,1,0:T(8,128)(2,1)}, bf16[12,64,512]{2,1,0:T(8,128)(2,1)S(1)}, u32[]{:S(2)}) copy-start(bf16[12,64,512]{2,1,0:T(8,128)(2,1)S(1)} %fusion.54) | copy-start | bytes 2359300
  236.1 8.7 %slice-start.8 = ((s8[4718592]{0:T(1024)(128)(4,1)}), s8[524288]{0:T(1024)(128)(4,1)S(1)}, s32[]{:S(2)}) async-start(s8[4718592]{0:T(1024)(128)(4,1)} %bitcast.139), calls=%async_computation.21 | async-start | bytes 1048576
  236.1 8.7 %slice-start.14 = ((s8[6291456]{0:T(1024)(128)(4,1)}), s8[4194304]{0:T(1024)(128)(4,1)S(1)}, s32[]{:S(2)}) async-start(s8[6291456]{0:T(1024)(128)(4,1)} %bitcast.145), calls=%async_computation.27 | async-start | bytes 8388608
  237.8 7.1 %slice-start.9 = ((s8[4718592]{0:T(1024)(128)(4,1)}), s8[4194304]{0:T(1024)(128)(4,1)S(1)}, s32[]{:S(2)}) async-start(s8[4718592]{0:T(1024)(128)(4,1)} %bitcast.139), calls=%async_computation.22 | async-start | bytes 8388608
  237.8 7.1 %slice-start.15 = ((s8[6291456]{0:T(1024)(128)(4,1)}), s8[2097152]{0:T(1024)(128)(4,1)S(1)}, s32[]{:S(2)}) async-start(s8[6291456]{0:T(1024)(128)(4,1)} %bitcast.145), calls=%async_computation.28 | async-start | bytes 4194304
  244.3 7.2 %slice-start.12 = ((s8[4718592]{0:T(1024)(128)(4,1)}), s8[4194304]{0:T(1024)(128)(4,1)S(1)}, s32[]{:S(2)}) async-start(s8[4718592]{0:T(1024)(128)(4,1)} %bitcast.143), calls=%async_computation.25 | async-start | bytes 8388608
  244.8 10.4 %copy-start.2 = (f32[512,768]{1,0:T(8,128)}, f32[512,768]{1,0:T(8,128)S(1)}, u32[]{:S(2)}) copy-start(f32[512,768]{1,0:T(8,128)S(1)} %get-tuple-element.59) | copy-start | bytes 4718596
  244.9 6.6 %slice-start.13 = ((s8[4718592]{0:T(1024)(128)(4,1)}), s8[524288]{0:T(1024)(128)(4,1)S(1)}, s32[]{:S(2)}) async-start(s8[4718592]{0:T(1024)(128)(4,1)} %bitcast.143), calls=%async_computation.26 | async-start | bytes 1048576
  259.1 4.5 copy-start.41
  259.1 111.9 %reduce-scatter.5.cloned.1.call-start = ((), (), s32[]{:S(2)}) async-start(), calls=%async_computation.8 | async-start | bytes 7962624 | tf_op jit(solution)/shard_map/reduce_scatter | solution.py:223
  263.6 11.0 %copy-start.44 = (bf16[512,768]{0,1:T(8,128)(2,1)}, bf16[512,768]{0,1:T(8,128)(2,1)S(1)}, u32[]{:S(2)}) copy-start(bf16[512,768]{0,1:T(8,128)(2,1)S(1)} %copy.83) | copy-start | bytes 2359300
  263.6 11.0 %slice-start = ((s8[12582912]{0:T(1024)(128)(4,1)}), s8[4194304]{0:T(1024)(128)(4,1)S(1)}, s32[]{:S(2)}) async-start(s8[12582912]{0:T(1024)(128)(4,1)} %bitcast.89), calls=%async_computation.13 | async-start | bytes 8388608
  263.6 12.4 %slice-start.1 = ((s8[12582912]{0:T(1024)(128)(4,1)}), s8[4194304]{0:T(1024)(128)(4,1)S(1)}, s32[]{:S(2)}) async-start(s8[12582912]{0:T(1024)(128)(4,1)} %bitcast.89), calls=%async_computation.14 | async-start | bytes 8388608
  263.6 13.6 %slice-start.2 = ((s8[12582912]{0:T(1024)(128)(4,1)}), s8[4194304]{0:T(1024)(128)(4,1)S(1)}, s32[]{:S(2)}) async-start(s8[12582912]{0:T(1024)(128)(4,1)} %bitcast.89), calls=%async_computation.15 | async-start | bytes 8388608
  277.2 6.8 %copy-start.11 = (bf16[512,768]{0,1:T(8,128)(2,1)S(1)}, bf16[512,768]{0,1:T(8,128)(2,1)}, u32[]{:S(2)}) copy-start(bf16[512,768]{0,1:T(8,128)(2,1)} %copy-done.10) | copy-start | bytes 2359300
  287.3 5.6 copy-start.8
  289.6 4.2 copy-start.1
  289.6 4.2 copy-start.53
  299.1 151.9 %reduce-scatter.11.cloned.1.call-start = ((), (), s32[]{:S(2)}) async-start(), calls=%async_computation.11 | async-start | bytes 10616832 | tf_op jit(solution)/shard_map/reduce_scatter | solution.py:232
  299.2 6.5 %copy-start.3 = (f32[512,768]{1,0:T(8,128)S(1)}, f32[512,768]{1,0:T(8,128)}, u32[]{:S(2)}) copy-start(f32[512,768]{1,0:T(8,128)} %copy-done.2) | copy-start | bytes 4718596
  317.3 213.7 %reduce-scatter.9.cloned.1.call-start = ((), (), s32[]{:S(2)}) async-start(), calls=%async_computation.10 | async-start | bytes 10616832 | tf_op jit(solution)/shard_map/reduce_scatter | solution.py:230
  318.0 6.0 copy-start.23
  330.0 282.0 %all-reduce.23.cloned.1.call-start = ((), (), s32[]{:S(2)}) async-start(), calls=%async_computation.12 | async-start | bytes 3538944 | tf_op jit(solution)/shard_map/psum | solution.py:235
  331.7 4.8 copy-start.60
  331.7 6.7 %copy-start.14 = (bf16[12,64,512]{2,1,0:T(8,128)(2,1)S(1)}, bf16[12,64,512]{2,1,0:T(8,128)(2,1)}, u32[]{:S(2)}) copy-start(bf16[12,64,512]{2,1,0:T(8,128)(2,1)} %copy-done.12) | copy-start | bytes 2359300
  331.7 6.7 %copy-start.30 = (bf16[12,64,512]{2,1,0:T(8,128)(2,1)S(1)}, bf16[12,64,512]{2,1,0:T(8,128)(2,1)}, u32[]{:S(2)}) copy-start(bf16[12,64,512]{2,1,0:T(8,128)(2,1)} %copy-done.28) | copy-start | bytes 2359300
  331.7 6.7 %copy-start.32 = (bf16[12,64,512]{2,1,0:T(8,128)(2,1)S(1)}, bf16[12,64,512]{2,1,0:T(8,128)(2,1)}, u32[]{:S(2)}) copy-start(bf16[12,64,512]{2,1,0:T(8,128)(2,1)} %copy-done.31) | copy-start | bytes 2359300
  331.7 6.7 %copy-start.37 = (bf16[12,64,512]{2,1,0:T(8,128)(2,1)S(1)}, bf16[12,64,512]{2,1,0:T(8,128)(2,1)}, u32[]{:S(2)}) copy-start(bf16[12,64,512]{2,1,0:T(8,128)(2,1)} %copy-done.35) | copy-start | bytes 2359300
  341.5 191.7 %copy-start.62 = (f32[3072]{0:T(1024)S(1)}, f32[3072]{0:T(1024)}, u32[]{:S(2)}) copy-start(f32[3072]{0:T(1024)} %get-tuple-element.60) | copy-start | bytes 36868
  341.5 191.7 %copy-start.66 = (f32[768]{0:T(1024)S(1)}, f32[768]{0:T(1024)}, u32[]{:S(2)}) copy-start(f32[768]{0:T(1024)} %get-tuple-element.24) | copy-start | bytes 9220
  341.5 191.8 %copy-start.65 = (f32[768]{0:T(1024)S(1)}, f32[768]{0:T(1024)}, u32[]{:S(2)}) copy-start(f32[768]{0:T(1024)} %get-tuple-element.17) | copy-start | bytes 9220
  341.5 191.8 %copy-start.61 = (f32[768]{0:T(1024)S(1)}, f32[768]{0:T(1024)}, u32[]{:S(2)}) copy-start(f32[768]{0:T(1024)} %get-tuple-element.64) | copy-start | bytes 9220
  341.5 234.7 %copy-start.4 = (f32[512,768]{1,0:T(8,128)S(1)}, f32[512,768]{1,0:T(8,128)}, u32[]{:S(2)}) copy-start(f32[512,768]{1,0:T(8,128)} %copy-done.2) | copy-start | bytes 4718596
  612.0 4.4 copy-start.48
  612.0 5.4 copy-start.49
  (34 other events, 61.9 us)
Sparse Core Ops, SparseCore 0:
  9.9 36.8 all-gather.5
  48.7 24.0 all-gather.7
  74.7 38.9 all-gather.9
  115.4 38.9 all-gather.11
  259.2 42.4 reduce-scatter.6
  305.5 65.4 reduce-scatter.4
  374.5 76.4 reduce-scatter.10
  454.5 76.4 reduce-scatter.8
  534.8 77.1 all-reduce.22
where the time goes:
time: 628 us; the launch traced here: 625 us
  waiting for transfers between devices  276 us (44%)
  matrix products  180 us (29%)
  blocking collectives  72 us (11%)
  other arithmetic  45.2 us (7%)
  local copies, waits for them, and re-layouts  34.1 us (5%)
  between operations  17.6 us (3%)
    reduce_scatter x1, waiting for transfers between devices, body(): lax.psum_scatter(summed[11], 'own', scatter_dimension=0, tiled=True)  78 us
    reduce_scatter x1, waiting for transfers between devices, body(): lax.psum_scatter(summed[9], 'own', scatter_dimension=0, tiled=True)  77.9 us
    unnamed x2, blocking collectives  50.4 us
    all_gather x1, waiting for transfers between devices, fetch(): lax.all_gather(shards[11], 'own', axis=0, tiled=True)  33.5 us
    all_gather x1, waiting for transfers between devices, fetch(): lax.all_gather(shards[9], 'own', axis=0, tiled=True)  31.4 us
    reduce_scatter x1, waiting for transfers between devices, body(): lax.psum_scatter(summed[2], 'own', scatter_dimension=0, tiled=True)  29.5 us
    unnamed x205, local copies, waits for them, and re-layouts  22.9 us
    psum x1, waiting for transfers between devices, body(): lax.psum(as_sent(owned), 'grp')  22.8 us
  transfers between devices with their start and end apart: 9, of which 6 were waited for; matrix products, arithmetic and copies ran while one was open for 23% of the time, Pallas kernels for 0%

commit v1 on v0

--- a/solution.py
+++ b/solution.py
@@ -1,14 +1,756 @@
+import functools
+
 import jax
 import jax.numpy as jnp
 from jax import lax
+from jax.experimental import pallas as pl
+from jax.experimental.pallas import tpu as pltpu
 from jax.sharding import PartitionSpec as P
 
 HEADS = 12
 HEAD_DIM = 64
 USES = 2
-
-
 EPSILON = 1e-05
+SCALE = HEAD_DIM ** (-0.5)
+TANH_SCALE = 0.7978845608028654
+TANH_CUBIC = 0.044715
+MESH = pl.DeviceIdType.MESH
+f32 = jnp.float32
+bf16 = jnp.bfloat16
+
+GAIN1, SHIFT1, BIAS_Q, BIAS_V, BIAS_OUT, GAIN2, SHIFT2, BIAS_PROJ, BIAS_FC = range(9)
+
+
+def dot(a, b, ca=1, cb=0):
+    return lax.dot_general(a, b, (((ca,), (cb,)), ((), ())), preferred_element_type=f32)
+
+
+def loop(count, body):
+    def step(i, carry):
+        body(i)
+        return carry
+
+    lax.fori_loop(0, count, step, 0)
+
+
+def span(begin, end, body):
+    def step(i, carry):
+        body(i)
+        return carry
+
+    lax.fori_loop(begin, end, step, 0)
+
+
+def part(i, size):
+    return pl.ds(pl.multiple_of(i * size, size), size)
+
+
+def centred(x):
+    centre = x - jnp.mean(x, axis=-1, keepdims=True)
+    spread = jnp.mean(centre * centre, axis=-1, keepdims=True)
+    return centre, lax.rsqrt(spread + EPSILON)
+
+
+def norm_forward(x, gain, shift, h):
+    rows = 128
+
+    def step(i):
+        centre, r = centred(x[part(i, rows), :].astype(f32))
+        h[part(i, rows), :] = (centre * r * gain + shift).astype(bf16)
+
+    loop(x.shape[0] // rows, step)
+
+
+def norm_backward(x, dh, gain, grad, out, sums, gain_row, shift_row, low=None):
+    rows = 128
+    sums[gain_row : gain_row + 1, :] = jnp.zeros_like(gain)
+    sums[shift_row : shift_row + 1, :] = jnp.zeros_like(gain)
+
+    def step(i):
+        centre, r = centred(x[part(i, rows), :].astype(f32))
+        n = centre * r
+        d = dh[part(i, rows), :]
+        sums[gain_row : gain_row + 1, :] += jnp.sum(d * n, axis=0, keepdims=True)
+        sums[shift_row : shift_row + 1, :] += jnp.sum(d, axis=0, keepdims=True)
+        e = d * gain
+        inner = e - jnp.mean(e, axis=-1, keepdims=True) - n * jnp.mean(e * n, axis=-1, keepdims=True)
+        result = grad[part(i, rows), :].astype(f32) + r * inner
+        out[part(i, rows), :] = result
+        if low is not None:
+            low[part(i, rows), :] = result.astype(bf16)
+
+    loop(x.shape[0] // rows, step)
+
+
+def column_sum(x):
+    return jnp.sum(x.astype(f32), axis=0, keepdims=True)
+
+
+def make_mask(doc, mask):
+    count = doc.shape[1]
+    half = count // 2
+    ids = doc[0:1, :].astype(f32)
+    keys = jnp.broadcast_to(ids, (128, count)).T[:, :1]
+    for k0, q0, place in ((0, 0, 0), (half, half, count)):
+        width = count - q0
+        row = lax.broadcasted_iota(jnp.int32, (half, width), 0) + k0
+        col = lax.broadcasted_iota(jnp.int32, (half, width), 1) + q0
+        key = keys[k0 : k0 + half]
+        same = (key == ids[:, q0:]) & (row <= col) & ((key != 0.0) | (row == col))
+        mask[:, place : place + width] = jnp.where(same, 0.0, -1e30)
+
+
+def head_lanes(h, x):
+    lane = lax.broadcasted_iota(jnp.int32, (1, 2 * HEAD_DIM), 1)
+    keep = (lane < HEAD_DIM) if h == 0 else (lane >= HEAD_DIM)
+    return jnp.where(keep, x, jnp.zeros_like(x))
+
+
+def attention_forward(qkv, mask, probs, o, begin=0, end=6):
+    count, width = o.shape
+    half = count // 2
+    pair = 2 * HEAD_DIM
+
+    def step(i):
+        col = part(i, pair)
+        q = qkv[:, col]
+        k = qkv[:, pl.ds(pl.multiple_of(width + i * pair, pair), pair)]
+        v = qkv[:, pl.ds(pl.multiple_of(2 * width + i * pair, pair), pair)]
+        vt = v.T
+        outs = []
+        for h in range(2):
+            kh = head_lanes(h, k)
+            s0 = dot(kh[:half], q, 1, 1) + mask[:, :count]
+            s1 = dot(kh[half:], q[half:], 1, 1) + mask[:, count:]
+            m0 = jnp.max(s0, axis=0, keepdims=True)
+            m1 = jnp.max(s1, axis=0, keepdims=True)
+            top = jnp.concatenate([m0[:, :half], jnp.maximum(m0[:, half:], m1)], axis=1)
+            e0 = jnp.exp(s0 - top)
+            e1 = jnp.exp(s1 - top[:, half:])
+            l0 = jnp.sum(e0, axis=0, keepdims=True)
+            l1 = jnp.sum(e1, axis=0, keepdims=True)
+            r = 1.0 / jnp.concatenate([l0[:, :half], l0[:, half:] + l1], axis=1)
+            p0 = (e0 * r).astype(bf16)
+            p1 = (e1 * r[:, half:]).astype(bf16)
+            probs[2 * i + h, :, :count] = p0
+            probs[2 * i + h, :, count:] = p1
+            vh = vt[h * HEAD_DIM : (h + 1) * HEAD_DIM]
+            first = dot(vh[:, :half], p0)
+            second = dot(vh[:, half:], p1)
+            outs.append(jnp.concatenate([first[:, :half], first[:, half:] + second], axis=1))
+        o[:, col] = jnp.concatenate(outs, axis=0).astype(bf16).T
+
+    span(begin, end, step)
+
+
+def attention_backward(qkv, probs, do, dz, sums):
+    count, width = do.shape
+    half = count // 2
+    pair = 2 * HEAD_DIM
+
+    def step(i):
+        cq = part(i, pair)
+        ck = pl.ds(pl.multiple_of(width + i * pair, pair), pair)
+        cv = pl.ds(pl.multiple_of(2 * width + i * pair, pair), pair)
+        q, k, v, d = qkv[:, cq], qkv[:, ck], qkv[:, cv], do[:, cq]
+        dq = dk = dv = None
+        for h in range(2):
+            dh, kh, qh = head_lanes(h, d), head_lanes(h, k), head_lanes(h, q)
+            p0 = probs[2 * i + h, :, :count]
+            p1 = probs[2 * i + h, :, count:]
+            d0 = dot(v[:half], dh, 1, 1)
+            d1 = dot(v[half:], dh[half:], 1, 1)
+            w0 = p0.astype(f32)
+            w1 = p1.astype(f32)
+            t0 = jnp.sum(d0 * w0, axis=0, keepdims=True)
+            t1 = jnp.sum(d1 * w1, axis=0, keepdims=True)
+            t = jnp.concatenate([t0[:, :half], t0[:, half:] + t1], axis=1)
+            s0 = (w0 * (d0 - t)).astype(bf16)
+            s1 = (w1 * (d1 - t[:, half:])).astype(bf16)
+            v_term = jnp.concatenate([dot(p0, dh), dot(p1, dh[half:])], axis=0)
+            k_term = jnp.concatenate([dot(s0, qh), dot(s1, qh[half:])], axis=0)
+            qa = dot(s0, kh[:half], 0, 0)
+            qb = dot(s1, kh[half:], 0, 0)
+            q_term = jnp.concatenate([qa[:half], qa[half:] + qb], axis=0)
+            dq = q_term if dq is None else dq + q_term
+            dk = k_term if dk is None else dk + k_term
+            dv = v_term if dv is None else dv + v_term
+        dq = (dq * SCALE).astype(bf16)
+        dv = dv.astype(bf16)
+        dz[:, cq] = dq
+        dz[:, ck] = dk.astype(bf16)
+        dz[:, cv] = dv
+        sums[BIAS_Q : BIAS_Q + 1, cq] = column_sum(dq)
+        sums[BIAS_V : BIAS_V + 1, cq] = column_sum(dv)
+
+    loop(width // pair, step)
+
+
+def small(block, row):
+    return block[row : row + 1, :]
+
+
+def hidden_forward(h2, wfc, block, f, slope, begin, end):
+    width = h2.shape[1]
+
+    def hidden(i):
+        col = part(i, width)
+        u = dot(h2[...], wfc[:, col]) + block[pl.ds(BIAS_FC + i, 1), :]
+        square = u * u
+        t = jnp.tanh(u * (TANH_SCALE + (TANH_SCALE * TANH_CUBIC) * square))
+        rise = 0.5 + 0.5 * t
+        f[:, col] = (u * rise).astype(bf16)
+        inner = TANH_SCALE + (3.0 * TANH_SCALE * TANH_CUBIC) * square
+        slope[:, col] = (rise + (0.5 * u) * (1.0 - t * t) * inner).astype(bf16)
+
+    span(begin, end, hidden)
+
+
+def forward_layer(x, block, weights, mask, kept, result, ready):
+    wqkv, wout, wfc, wproj = weights
+    h1, qkv, probs, o, x1, h2, slope, f = kept
+    width = x.shape[1]
+    ready("small")
+    norm_forward(x, small(block, GAIN1), small(block, SHIFT1), h1)
+    ready("qkv")
+    h = h1[...]
+    qkv[:, :width] = (dot(h, wqkv[:, :width]) + small(block, BIAS_Q)).astype(bf16) * SCALE
+    qkv[:, width : 2 * width] = dot(h, wqkv[:, width : 2 * width]).astype(bf16)
+    qkv[:, 2 * width :] = (dot(h, wqkv[:, 2 * width :]) + small(block, BIAS_V)).astype(bf16)
+    attention_forward(qkv, mask, probs, o)
+    ready("out")
+    x1[...] = x[...].astype(f32) + (dot(o[...], wout[...]) + small(block, BIAS_OUT))
+    norm_forward(x1, small(block, GAIN2), small(block, SHIFT2), h2)
+    ready("fc")
+
+    hidden_forward(h2, wfc, block, f, slope, 0, wfc.shape[1] // width)
+    ready("proj")
+    result[...] = x1[...] + (dot(f[...], wproj[...]) + small(block, BIAS_PROJ))
+
+
+def backward_hidden(gm, wproj, slope, du, sums):
+    width = gm.shape[1]
+
+    def hidden(i):
+        col = part(i, width)
+        d = (dot(gm[...], wproj[col, :], 1, 1) * slope[:, col].astype(f32)).astype(bf16)
+        du[:, col] = d
+        sums[pl.ds(BIAS_FC + i, 1), :] = column_sum(d)
+
+    loop(wproj.shape[0] // width, hidden)
+
+
+def backward_layer(x, grad, gm, block, weights, kept, scratch, result, sums, done):
+    wqkv, wout, wfc, wproj = weights
+    qkv, probs, x1, slope = kept
+    dh, do, da = scratch
+    sums[BIAS_PROJ : BIAS_PROJ + 1, :] = column_sum(gm[...])
+    backward_hidden(gm, wproj, slope, slope, sums)
+    done("du")
+    dh[...] = dot(slope[...], wfc[...], 1, 1)
+    norm_backward(x1, dh, small(block, GAIN2), grad, result, sums, GAIN2, SHIFT2, da)
+    done("da")
+    sums[BIAS_OUT : BIAS_OUT + 1, :] = column_sum(da[...])
+    do[...] = dot(da[...], wout[...], 1, 1).astype(bf16)
+    attention_backward(qkv, probs, do, qkv, sums)
+    done("dz")
+    dh[...] = dot(qkv[...], wqkv[...], 1, 1)
+    norm_backward(x, dh, small(block, GAIN1), result, result, sums, GAIN1, SHIFT1)
+
+
+def coords():
+    own = lax.axis_index("own")
+    return lax.axis_index("grp"), own // 2, lax.rem(own, 2)
+
+
+class Unit:
+    def __init__(self, shard, full, row, rows, col, cols):
+        self.shard, self.full = shard, full
+        self.row, self.rows, self.col, self.cols = row, rows, col, cols
+
+    def mine(self, half=None):
+        rows = self.rows if half is None else self.rows // 2
+        start = self.row + (0 if half is None else half * rows)
+        return self.shard.at[pl.ds(start, rows), pl.ds(self.col, self.cols)]
+
+    def block(self, owner, half=None):
+        rows = self.rows if half is None else self.rows // 2
+        start = owner * self.shard.shape[0] + self.row + (0 if half is None else half * rows)
+        return self.full.at[pl.ds(pl.multiple_of(start, 16), rows), pl.ds(self.col, self.cols)]
+
+
+PIECES = [(1, 0), (1, 1), (2, 0), (2, 1), (3, 0), (3, 1)]
+
+
+class Gather:
+    def __init__(self, units, link_send, link_recv, core_send, core_recv, own_sem):
+        self.units = units
+        self.link_send, self.link_recv = link_send, link_recv
+        self.core_send, self.core_recv, self.own_sem = core_send, core_recv, own_sem
+        self.grp, self.chip, self.core = coords()
+        self.odd = lax.rem(self.grp, 2)
+        self.sent = []
+
+    def owner(self, offset):
+        return jnp.bitwise_xor(self.chip, offset) * 2 + self.core
+
+    def device(self, chip_offset, along_z=False):
+        own = jnp.bitwise_xor(self.chip, chip_offset) * 2 + self.core
+        grp = self.grp + 1 - 2 * self.odd if along_z else self.grp
+        return (grp, own)
+
+    def link(self, k, src, dst, piece, out, device):
+        return pltpu.make_async_remote_copy(
+            src_ref=src,
+            dst_ref=dst,
+            send_sem=self.link_send.at[k, out],
+            recv_sem=self.link_recv.at[k, piece],
+            device_id=device,
+            device_id_type=MESH,
+        )
+
+    def across(self, k, src, dst, slot):
+        return pltpu.make_async_remote_copy(
+            src_ref=src,
+            dst_ref=dst,
+            send_sem=self.core_send.at[k, slot],
+            recv_sem=self.core_recv.at[k, slot],
+            device_id=(self.grp, self.chip * 2 + 1 - self.core),
+            device_id_type=MESH,
+        )
+
+    def own(self, k):
+        unit = self.units[k]
+        return pltpu.make_async_copy(unit.mine(), unit.block(self.owner(0)), self.own_sem.at[k])
+
+    def first(self, k, offset, half, out):
+        unit = self.units[k]
+        piece = PIECES.index((offset, half))
+        return self.link(
+            k, unit.mine(half), unit.block(self.owner(0), half), piece, out, self.device(offset)
+        )
+
+    def relay(self, k, offset, half, way, out):
+        unit = self.units[k]
+        piece = unit.block(self.owner(offset), half)
+        return self.link(k, piece, piece, PIECES.index((3, half)), out, self.device(way))
+
+    def pair(self, k, offset, half, out):
+        unit = self.units[k]
+        piece = unit.block(self.owner(offset), half)
+        return self.link(k, piece, piece, PIECES.index((offset, half)), out, self.device(0, True))
+
+    def hand(self, k, offset, half):
+        unit = self.units[k]
+        piece = unit.block(self.owner(offset), half)
+        return self.across(k, piece, piece, PIECES.index((offset, half)))
+
+    def arrived(self, k, offset, half):
+        unit = self.units[k]
+        piece = unit.block(self.owner(offset), half)
+        self.link(k, piece, piece, PIECES.index((offset, half)), 0, self.device(1)).wait_recv()
+
+    def plan(self, k):
+        even = [
+            self.first(k, 1, 0, 0),
+            self.first(k, 2, 1, 1),
+            self.first(k, 1, 1, 2),
+            self.first(k, 2, 0, 3),
+            self.pair(k, 1, 0, 4),
+            self.pair(k, 2, 1, 5),
+        ]
+        odd = [
+            self.first(k, 1, 1, 0),
+            self.first(k, 2, 0, 1),
+            self.relay(k, 2, 0, 1, 2),
+            self.relay(k, 1, 1, 2, 3),
+            self.pair(k, 3, 0, 4),
+            self.pair(k, 3, 1, 5),
+        ]
+        return even, odd
+
+    def start(self, k):
+        even, odd = self.plan(k)
+
+        @pl.when(self.odd == 0)
+        def _():
+            for copy in even[:4]:
+                copy.start()
+
+        @pl.when(self.odd == 1)
+        def _():
+            for copy in odd[:2]:
+                copy.start()
+
+        unit = self.units[k]
+        self.across(k, unit.mine(), unit.block(self.owner(0)), len(PIECES)).start()
+        self.own(k).start()
+
+    def serve_first(self, k):
+        even, odd = self.plan(k)
+
+        @pl.when(self.odd == 0)
+        def _():
+            for at, (offset, half) in enumerate(((1, 0), (2, 1), (1, 1), (2, 0))):
+                self.arrived(k, offset, half)
+                if at < 2:
+                    even[4 + at].start()
+                self.hand(k, offset, half).start()
+
+        @pl.when(self.odd == 1)
+        def _():
+            for at, (offset, half) in enumerate(((2, 0), (1, 1))):
+                self.arrived(k, offset, half)
+                odd[2 + at].start()
+                self.hand(k, offset, half).start()
+
+    def serve_second(self, k):
+        even, odd = self.plan(k)
+
+        @pl.when(self.odd == 0)
+        def _():
+            for half in range(2):
+                self.arrived(k, 3, half)
+                self.hand(k, 3, half).start()
+
+        @pl.when(self.odd == 1)
+        def _():
+            for half in range(2):
+                self.arrived(k, 3, half)
+                odd[4 + half].start()
+                self.hand(k, 3, half).start()
+            for offset, half in ((1, 0), (2, 1)):
+                self.arrived(k, offset, half)
+                self.hand(k, offset, half).start()
+
+    def finish(self, k):
+        unit = self.units[k]
+        other = 1 - 2 * self.core
+        self.own(k).wait()
+        whole = unit.block(self.owner(0) + other)
+        self.across(k, whole, whole, len(PIECES)).wait_recv()
+        for slot, (offset, half) in enumerate(PIECES):
+            piece = unit.block(self.owner(offset) + other, half)
+            self.across(k, piece, piece, slot).wait_recv()
+
+    def drain(self, k):
+        even, odd = self.plan(k)
+
+        @pl.when(self.odd == 0)
+        def _():
+            for copy in even:
+                copy.wait_send()
+
+        @pl.when(self.odd == 1)
+        def _():
+            for copy in odd:
+                copy.wait_send()
+
+        unit = self.units[k]
+        self.across(k, unit.mine(), unit.block(self.owner(0)), len(PIECES)).wait_send()
+        for offset, half in PIECES:
+            self.hand(k, offset, half).wait_send()
+
+
+def store(copies, sem, src, dst):
+    copy = pltpu.make_async_copy(src, dst, sem.at[len(copies)])
+    copy.start()
+    copies.append(copy)
+
+
+def first_kernel(
+    tokens, doc, packed, sqkv, sout, sfc, sproj,
+    x2_out, block_out, mask_out, wqkv_out, wout_out, wfc_out, wproj_out,
+    h1_out, qkv_out, probs_out, o_out, x1_out, h2_out, slope_out, f_out,
+    wqkv, wout, wfc, wproj, block, mask, h1, qkv, probs, o, x1, h2, slope, f, x2, many,
+    link_send, link_recv, core_send, core_recv, own_sem, small_send, small_recv, out_sem,
+):
+    grp, chip, core = coords()
+    me = chip * 2 + core
+    width = tokens.shape[1]
+    barrier = pltpu.get_barrier_semaphore()
+    peers = [(grp, jnp.bitwise_xor(me, j)) for j in range(1, 8)]
+    peers.append((grp + 1 - 2 * lax.rem(grp, 2), me))
+    for peer in peers:
+        pl.semaphore_signal(barrier, inc=1, device_id=peer, device_id_type=MESH)
+    pl.semaphore_wait(barrier, len(peers))
+
+    units = [Unit(sqkv, wqkv, 0, sqkv.shape[0], i * width, width) for i in range(3)]
+    units += [Unit(sout, wout, 0, sout.shape[0], 0, width)]
+    units += [Unit(sfc, wfc, 0, sfc.shape[0], i * width, width) for i in range(sfc.shape[1] // width)]
+    thirds = sproj.shape[0] // 3
+    units += [Unit(sproj, wproj, i * thirds, thirds, 0, width) for i in range(3)]
+    gather = Gather(units, link_send, link_recv, core_send, core_recv, own_sem)
+    count = len(units)
+
+    def small_copy(j, slot):
+        return pltpu.make_async_remote_copy(
+            src_ref=packed,
+            dst_ref=many.at[slot],
+            send_sem=small_send.at[j - 1],
+            recv_sem=small_recv.at[j - 1],
+            device_id=(grp, jnp.bitwise_xor(me, j)),
+            device_id_type=MESH,
+        )
+
+    for j in range(1, 8):
+        small_copy(j, j).start()
+    gather.start(0)
+    gather.start(1)
+    copies = []
+
+    def slot(s):
+        if s < count:
+            gather.serve_first(s)
+        if s + 2 < count:
+            gather.start(s + 2)
+        if 0 <= s - 1 < count:
+            gather.serve_second(s - 1)
+        if 0 <= s - 2 < count:
+            gather.finish(s - 2)
+
+    make_mask(doc, mask)
+    store(copies, out_sem, mask, mask_out)
+    total = packed[...].astype(f32)
+    for j in range(1, 8):
+        small_copy(j, j).wait_recv()
+        total = total + many[j].astype(f32)
+    block[...] = total
+    store(copies, out_sem, block, block_out)
+    norm_forward(tokens, small(block, GAIN1), small(block, SHIFT1), h1)
+    store(copies, out_sem, h1, h1_out)
+    for s in range(3):
+        slot(s)
+    h = h1[...]
+    qkv[:, :width] = (dot(h, wqkv[:, :width]) + small(block, BIAS_Q)).astype(bf16) * SCALE
+    slot(3)
+    qkv[:, width : 2 * width] = dot(h1[...], wqkv[:, width : 2 * width]).astype(bf16)
+    slot(4)
+    store(copies, out_sem, wqkv, wqkv_out)
+    qkv[:, 2 * width :] = (dot(h1[...], wqkv[:, 2 * width :]) + small(block, BIAS_V)).astype(bf16)
+    store(copies, out_sem, qkv, qkv_out)
+    attention_forward(qkv, mask, probs, o, 0, 2)
+    slot(5)
+    store(copies, out_sem, wout, wout_out)
+    attention_forward(qkv, mask, probs, o, 2, 4)
+    slot(6)
+    attention_forward(qkv, mask, probs, o, 4, 6)
+    store(copies, out_sem, probs, probs_out)
+    store(copies, out_sem, o, o_out)
+    x1[...] = tokens[...].astype(f32) + (dot(o[...], wout[...]) + small(block, BIAS_OUT))
+    norm_forward(x1, small(block, GAIN2), small(block, SHIFT2), h2)
+    store(copies, out_sem, x1, x1_out)
+    store(copies, out_sem, h2, h2_out)
+    slot(7)
+    hidden_forward(h2, wfc, block, f, slope, 0, 2)
+    slot(8)
+    hidden_forward(h2, wfc, block, f, slope, 2, 3)
+    slot(9)
+    store(copies, out_sem, wfc, wfc_out)
+    hidden_forward(h2, wfc, block, f, slope, 3, 4)
+    store(copies, out_sem, f, f_out)
+    store(copies, out_sem, slope, slope_out)
+
+    def project(i):
+        rows = [pl.ds(owner * sproj.shape[0] + i * thirds, thirds) for owner in range(8)]
+        left = jnp.concatenate([f[:, at] for at in rows], axis=1)
+        right = jnp.concatenate([wproj[at, :] for at in rows], axis=0)
+        return dot(left, right)
+
+    slot(10)
+    x2[...] = x1[...] + (project(0) + small(block, BIAS_PROJ))
+    slot(11)
+    x2[...] += project(1)
+    slot(12)
+    store(copies, out_sem, wproj, wproj_out)
+    x2[...] += project(2)
+    store(copies, out_sem, x2, x2_out)
+    for k in range(count):
+        gather.drain(k)
+    for j in range(1, 8):
+        small_copy(j, j).wait_send()
+    for copy in copies:
+        copy.wait()
+
+
+def fetch(copies, src, dst, sem):
+    copy = pltpu.make_async_copy(src, dst, sem)
+    copy.start()
+    copies.append(copy)
+    return copy
+
+
+def second_kernel(
+    x_in, cot_in, block, mask_in, wqkv_in, wout_in, wfc_in, wproj_in,
+    act_out, grad_out, sums, h1_out, dz_out, o_out, da_out, h2_out, du_out, f_out,
+    x, cot, mask, wqkv, wout, wfc, wproj, h1, qkv, probs, o, x1, h2, slope, f, x2, dh, do, da, act, in_sem, out_sem,
+):
+    loads = []
+    for src, dst in (
+        (x_in, x), (mask_in, mask), (wqkv_in, wqkv), (wout_in, wout), (wfc_in, wfc), (wproj_in, wproj), (cot_in, cot)
+    ):
+        fetch(loads, src, dst, in_sem.at[len(loads)])
+    x_here, mask_here, qkv_here, out_here, fc_here, proj_here, cot_here = loads
+    waits = {"small": x_here, "qkv": qkv_here, "out": out_here, "fc": fc_here, "proj": proj_here}
+    copies = []
+    mask_here.wait()
+    forward_layer(
+        x, block, (wqkv, wout, wfc, wproj), mask, (h1, qkv, probs, o, x1, h2, slope, f), x2,
+        lambda name: waits[name].wait(),
+    )
+    for src, dst in ((h1, h1_out), (o, o_out), (h2, h2_out), (f, f_out)):
+        store(copies, out_sem, src, dst)
+    act[...] = x2[...].astype(bf16)
+    store(copies, out_sem, act, act_out)
+    cot_here.wait()
+    sums[...] = jnp.zeros_like(sums)
+    backward_layer(
+        x, cot, cot, block, (wqkv, wout, wfc, wproj), (qkv, probs, x1, slope), (dh, do, da), x2, sums,
+        lambda name: store(copies, out_sem, *{"du": (slope, du_out), "da": (da, da_out), "dz": (qkv, dz_out)}[name]),
+    )
+    store(copies, out_sem, x2, grad_out)
+    for copy in copies:
+        copy.wait()
+
+
+def third_kernel(
+    x_in, grad_in, block, wqkv_in, wout_in, wfc_in, wproj_in, qkv_in, probs_in, x1_in, slope_in,
+    grad_out, sums, gm_out, dz_out, da_out, du_out,
+    x, grad, wqkv, wout, wfc, wproj, qkv, probs, x1, slope, dh, do, da, gm, in_sem, out_sem,
+):
+    loads = []
+    for src, dst in (
+        (grad_in, grad), (wproj_in, wproj), (slope_in, slope), (wfc_in, wfc), (x1_in, x1), (wout_in, wout),
+        (qkv_in, qkv), (probs_in, probs), (wqkv_in, wqkv), (x_in, x),
+    ):
+        fetch(loads, src, dst, in_sem.at[len(loads)])
+    copies = []
+    for copy in loads:
+        copy.wait()
+    sums[...] = jnp.zeros_like(sums)
+    gm[...] = grad[...].astype(bf16)
+    store(copies, out_sem, gm, gm_out)
+    backward_layer(
+        x, grad, gm, block, (wqkv, wout, wfc, wproj), (qkv, probs, x1, slope), (dh, do, da), grad, sums,
+        lambda name: store(copies, out_sem, *{"du": (slope, du_out), "da": (da, da_out), "dz": (qkv, dz_out)}[name]),
+    )
+    store(copies, out_sem, grad, grad_out)
+    for copy in copies:
+        copy.wait()
+
+
+VMEM_BYTES = 62 * 2**20
+
+
+def spec(shape, dtype):
+    return jax.ShapeDtypeStruct(shape, dtype)
+
+
+def kernels_body(*args):
+    tokens, doc, cotangent = args[:3]
+    gain1, shift1, sqkv, bq, bv, sout, bo, gain2, shift2, sfc, bfc, sproj, bp = args[3:]
+    count, width = tokens.shape
+    ff = sfc.shape[1]
+    owners = lax.axis_size("own")
+    me = lax.axis_index("own")
+    rows = [gain1, shift1, bq, bv, bo, gain2, shift2, bp]
+    stacked = jnp.tile(jnp.stack(rows), (1, owners))
+    mine = lax.broadcasted_iota(jnp.int32, stacked.shape, 1) // gain1.shape[0] == me
+    stacked = jnp.where(mine, stacked, jnp.zeros_like(stacked))
+    tiled = jnp.tile(bfc, owners)
+    mine = lax.broadcasted_iota(jnp.int32, tiled.shape, 0) // bfc.shape[0] == me
+    tiled = jnp.where(mine, tiled, jnp.zeros_like(tiled)).reshape(ff // width, width)
+    packed = jnp.concatenate([stacked, tiled, jnp.zeros((16 - 8 - ff // width, width), bf16)])
+
+    hbm = pl.BlockSpec(memory_space=pl.ANY)
+    vmem = pl.BlockSpec(memory_space=pltpu.VMEM)
+    V = pltpu.VMEM
+    half = count // 2
+    x_s = ((count, width), f32)
+    low_s = ((count, width), bf16)
+    qkv_s = ((count, 3 * width), bf16)
+    ff_s = ((count, ff), bf16)
+    probs_s = ((HEADS, half, count + half), bf16)
+    mask_s = ((half, count + half), f32)
+    block_s = ((16, width), f32)
+    w_s = [((width, 3 * width), bf16), ((width, width), bf16), ((width, ff), bf16), ((ff, width), bf16)]
+    units = 3 + 1 + ff // width + 3
+    dma = pltpu.SemaphoreType.DMA
+
+    def call(kernel, inputs, outs, scratch, in_specs, out_specs, **params):
+        return pl.pallas_call(
+            kernel,
+            out_shape=[spec(*s) for s in outs],
+            in_specs=in_specs,
+            out_specs=out_specs,
+            scratch_shapes=scratch,
+            compiler_params=pltpu.CompilerParams(vmem_limit_bytes=VMEM_BYTES, **params),
+        )(*inputs)
+
+    outs = [x_s, block_s, mask_s, *w_s, low_s, qkv_s, probs_s, low_s, x_s, low_s, ff_s, ff_s]
+    (x2, block, mask, wqkv, wout, wfc, wproj, h1a, qkva, probsa, oa, x1a, h2a, slopea, fa) = call(
+        first_kernel,
+        (tokens, doc.reshape(1, count), packed, sqkv, sout, sfc, sproj),
+        outs,
+        [V(*s) for s in w_s]
+        + [V(*s) for s in (block_s, mask_s, low_s, qkv_s, probs_s, low_s, x_s, low_s, ff_s, ff_s, x_s)]
+        + [V((8, 16, width), bf16)]
+        + [dma((units, 6)), dma((units, 6)), dma((units, 7)), dma((units, 7)), dma((units,)), dma((7,)), dma((7,))]
+        + [dma((len(outs),))],
+        [vmem] * 3 + [hbm] * 4,
+        [hbm] * len(outs),
+        collective_id=0,
+        has_side_effects=True,
+    )
+    outs = [low_s, x_s, block_s, low_s, qkv_s, low_s, low_s, low_s, ff_s, ff_s]
+    act, grad, sumsb, h1b, dzb, ob, dab, h2b, dub, fb = call(
+        second_kernel,
+        (x2, cotangent, block, mask, wqkv, wout, wfc, wproj),
+        outs,
+        [V(*s) for s in (x_s, low_s, mask_s, *w_s, low_s, qkv_s, probs_s, low_s, x_s, low_s, ff_s, ff_s, x_s, x_s)]
+        + [V(*s) for s in (low_s, low_s, low_s)]
+        + [dma((7,)), dma((9,))],
+        [hbm, hbm, vmem, hbm, hbm, hbm, hbm, hbm],
+        [hbm, hbm, vmem] + [hbm] * 7,
+    )
+    outs = [x_s, block_s, low_s, qkv_s, low_s, ff_s]
+    tokens_grad, sumsa, gma, dza, daa, dua = call(
+        third_kernel,
+        (tokens, grad, block, wqkv, wout, wfc, wproj, qkva, probsa, x1a, slopea),
+        outs,
+        [V(*s) for s in (low_s, x_s, *w_s, qkv_s, probs_s, x_s, ff_s, x_s, low_s, low_s, low_s)]
+        + [dma((10,)), dma((5,))],
+        [hbm, hbm, vmem] + [hbm] * 8,
+        [hbm, vmem] + [hbm] * 4,
+    )
+
+    def term(xa, ya, xb, yb):
+        return jnp.einsum("td,te->de", xa, ya, preferred_element_type=f32) + jnp.einsum(
+            "td,te->de", xb, yb, preferred_element_type=f32
+        )
+
+    full = [
+        term(h1a, dza, h1b, dzb),
+        term(oa, daa, ob, dab),
+        term(h2a, dua, h2b, dub),
+        term(fa, gma, fb, cotangent),
+    ]
+    final = [
+        lax.psum(lax.psum_scatter(w.astype(bf16), "own", scatter_dimension=0, tiled=True), "grp").astype(f32)
+        for w in full
+    ]
+    sums = lax.psum(sumsa + sumsb, ("grp", "own"))
+
+    def own(row):
+        return lax.dynamic_slice(sums, (row, me * gain1.shape[0]), (1, gain1.shape[0]))[0]
+
+    bfc_grad = lax.dynamic_slice(
+        sums[BIAS_FC : BIAS_FC + ff // width].reshape(ff), (me * bfc.shape[0],), (bfc.shape[0],)
+    )
+    return (
+        act, tokens_grad, own(GAIN1), own(SHIFT1), final[0], own(BIAS_Q), own(BIAS_V), final[1], own(BIAS_OUT),
+        own(GAIN2), own(SHIFT2), final[2], bfc_grad, final[3], own(BIAS_PROJ),
+    )
 
 
 def as_sent(shard):
@@ -33,7 +775,7 @@
     return same & (col <= row) & ((doc[None, :] != 0) | (row == col))
 
 
-def forward_layer(x, weights, mask):
+def plain_forward(x, weights, mask):
     (
         gain_one,
         shift_one,
@@ -76,7 +818,7 @@
     return (result, kept)
 
 
-def backward_layer(x, weights, mask, grad):
+def plain_backward(x, weights, mask, grad):
     (
         gain_one,
         shift_one,
@@ -92,7 +834,7 @@
         w_proj,
         bias_proj,
     ) = weights
-    result, kept = forward_layer(x, weights, mask)
+    result, kept = plain_forward(x, weights, mask)
     h_one, query, key, value, probs, probs_low, mixed, middle, h_two, inner, active = kept
     width = w_qkv.shape[0]
     count = x.shape[0]
@@ -152,7 +894,7 @@
     return (d_middle + d_input, terms)
 
 
-def body(
+def plain_body(
     tokens,
     doc_ids,
     cotangent,
@@ -208,11 +950,11 @@
     saved = []
     for use in range(USES):
         saved.append(current)
-        current, kept = forward_layer(current, fetch(), mask)
+        current, kept = plain_forward(current, fetch(), mask)
     grad = cotangent.astype(jnp.float32)
     summed = None
     for use in reversed(range(USES)):
-        grad, terms = backward_layer(saved[use], fetch(), mask, grad)
+        grad, terms = plain_backward(saved[use], fetch(), mask, grad)
         if summed is None:
             summed = terms
         else:
@@ -238,7 +980,7 @@
 
 def solution(mesh):
     return jax.shard_map(
-        body,
+        kernels_body if tuple(mesh.axis_sizes) == (4, 8) else plain_body,
         mesh=mesh,
         in_specs=(
             P(("grp", "own"), None),

time: 628 us -> 470 us (0.75)
  matrix products: 180 us -> 27.4 us
  Pallas kernels: 0 us -> 152 us
  waiting for transfers between devices: 276 us -> 213 us
  other arithmetic: 45.2 us -> 6.79 us
  blocking collectives: 72 us -> 42.7 us
  local copies, waits for them, and re-layouts: 34.1 us -> 6.68 us
    pallas_call x0 -> x3, Pallas kernels: none -> 152 us  [call(): pl.pallas_call(kernel, out_shape=[spec(*s) for s in outs], in_specs=in_sp...]
    dot_general x34 -> x8, matrix products: 159 us -> 27.4 us  [the longest x4 15.3 us: term(): jnp.einsum('td,te->de', xb, yb, preferred_element_type=f32)]
    all_gather x4 -> x0, waiting for transfers between devices: 65 us -> none  [the longest x1 33.5 us: fetch(): lax.all_gather(shards[11], 'own', axis=0, tiled=True)]
    unnamed x2 -> x0, blocking collectives: 50.4 us -> none
    psum x1, blocking collectives: 13.1 us -> 42.7 us  [kernels_body(): sums = lax.psum(sumsa + sumsb, ('grp', 'own'))]
    convert_element_type x28 -> x4, other arithmetic: 32.7 us -> 6.1 us  [kernels_body(): lax.psum(lax.psum_scatter(w.astype(bf16), 'own', scatter_dimension=0, til...]
    sub x2 -> x0, matrix products: 20.6 us -> none  [forward_layer(): probs = jax.nn.softmax(scores, axis=-1)]
    unnamed x205 -> x34, local copies, waits for them, and re-layouts: 22.9 us -> 3.79 us
  transfers between devices with their start and end apart: 9 -> 5, of which waited for: 6 -> 5; matrix products, arithmetic and copies ran while one was open for 23% -> 5% of each run, Pallas kernels for 0% -> 0%
where the time goes in v1:
time: 470 us; the launch traced here: 464 us
  waiting for transfers between devices  213 us (45%)
  Pallas kernels  152 us (32%)
  blocking collectives  42.7 us (9%)
  matrix products  27.4 us (6%)
  between operations  14.5 us (3%)
  other arithmetic  6.79 us (1%)
  local copies, waits for them, and re-layouts  6.68 us (1%)
    reduce_scatter x4, waiting for transfers between devices, kernels_body(): lax.psum_scatter(w.astype(bf16), 'own', scatter_dimension=0, tiled=True)  177 us
    pallas_call x3, Pallas kernels, call(): pl.pallas_call(kernel, out_shape=[spec(*s) for s in outs], in_specs=in_sp...  152 us
    psum x1, blocking collectives, kernels_body(): sums = lax.psum(sumsa + sumsb, ('grp', 'own'))  42.7 us
    psum x1, waiting for transfers between devices, kernels_body(): lax.psum(lax.psum_scatter(w.astype(bf16), 'own', scatter_dimension=0, til...  36.3 us
    dot_general x4, matrix products, term(): jnp.einsum('td,te->de', xb, yb, preferred_element_type=f32)  15.3 us
    dot_general x4, matrix products, term(): jnp.einsum('td,te->de', xa, ya, preferred_element_type=f32)  12.1 us
  transfers between devices with their start and end apart: 5, of which 5 were waited for; matrix products, arithmetic and copies ran while one was open for 5% of the time, Pallas kernels for 0%

profile of v1, /device:TPU:0, one launch (start us, length us, event | category | flops | bytes accessed | tf_op | source)
XLA Modules:
  0.0 463.6 jit_solution(4534519037844920276)
XLA Ops:
  7.2 0.0 reduce-scatter.7.cloned.1.call-start
  7.3 0.8 stack.35
  8.1 0.1 tile.21
  8.2 0.7 tile.22
  8.9 0.6 pad_maximum_fusion.packed
  9.6 73.9 %shard_map.271 = (f32[512,768]{1,0:T(8,128)}, f32[16,768]{1,0:T(8,128)}, f32[256,768]{1,0:T(8,128)}, bf16[768,2304]{1,0:T(8,128)(2,1)}, bf16[768,768]{1,0:T(8,12...) custom-call(bf16[512,768]{1,0:T(8,128)(2,1)} %x_in.1, ...), custom_call_target="tpu_custom_call" | custom-call | tf_op jit(solution)/shard_map/pallas_call | solution.py:681
  83.5 45.3 %shard_map.272 = (bf16[512,768]{1,0:T(8,128)(2,1)}, f32[512,768]{1,0:T(8,128)}, f32[16,768]{1,0:T(8,128)}, bf16[512,768]{1,0:T(8,128)(2,1)}, bf16[512,2304]{1,0:...) custom-call(f32[512,768]{1,0:T(8,128)} %get-tuple-element.46.x_in, ...), custom_call_target="tpu_custom_call" | custom-call | tf_op jit(solution)/shard_map/pallas_call | solution.py:681
  128.8 0.0 copy-start.2
  128.8 32.7 %shard_map.273 = (f32[512,768]{1,0:T(8,128)}, f32[16,768]{1,0:T(8,128)}, bf16[512,768]{1,0:T(8,128)(2,1)}, bf16[512,2304]{1,0:T(8,128)(2,1)}, bf16[512,768]{1,0:T(8,128)(2,1)}, /*index=5*/bf16[512,3072]{1,0:T(8,128)(2,1)}) custom-call(bf16[512,768]{1,0:T(8,128)(2,1)} %x_in.1, f32[512,768]{1,0:T(8,128)} %get-tuple-element.54.grad_in, ...), custom_call_target="tpu_custom_call" | custom-call | tf_op jit(solution)/shard_map/pallas_call | solution.py:681
  161.5 0.0 copy-start.5
  161.5 0.0 copy-start.6
  161.5 0.0 copy-done.2
  161.5 2.1 fusion.8
  163.5 0.0 copy-done.5
  163.6 0.0 copy-done.6
  163.6 0.0 copy-start.1
  163.6 0.0 copy-start.4
  163.6 1.9 add_convert_fusion.3
  165.4 0.0 reduce-scatter.7.cloned.1.call-update
  165.5 0.0 reduce-scatter.5.cloned.1.call-start
  165.5 0.0 copy-done.1
  165.5 0.1 copy-done.4
  165.6 0.0 copy-start.14
  165.6 0.0 copy-start.16
  165.6 2.0 fusion.7
  167.6 0.0 copy-done.14
  167.6 0.0 copy-done.16
  167.6 4.1 add_convert_fusion.2
  171.7 0.0 copy-start.12
  171.8 0.0 reduce-scatter.5.cloned.1.call-update
  171.8 0.0 reduce-scatter.11.cloned.1.call-start
  171.8 1.9 copy-done.12
  173.7 0.0 copy-start.3
  173.7 0.0 copy-start.13
  173.7 4.0 fusion.10
  177.7 0.0 copy-done.3
  177.7 0.0 copy-done.13
  177.8 4.8 %add_convert_fusion = bf16[3072,768]{1,0:T(8,128)(2,1)} fusion(f32[3072,768]{1,0:T(8,128)S(1)} %fusion.10, bf16[512,3072]{1,0:T(8,128)(2,1)S(1)} %copy-done.13, bf16[512,768]{1,0:T(8,128)(2,1)S(1)} %copy-done.3), kind=kOutput, calls=%fused_computation | convolution fusion | flops 2420637696 | bytes 18087936 | tf_op jit(solution)/shard_map/td,te->de/dot_general | solution.py:728
  182.6 0.0 reduce-scatter.11.cloned.1.call-update
  182.6 0.0 reduce-scatter.9.cloned.1.call-start
  182.6 1.8 copy-done
  184.5 4.0 fusion.9
  188.5 0.0 copy-done.11
  188.5 0.0 copy-done.15
  188.5 4.6 add_convert_fusion.1
  193.0 0.0 reduce-scatter.9.cloned.1.call-update
  193.1 0.0 all-reduce.3.cloned.1.call-start
  193.1 10.1 %reduce-scatter.7.cloned.1.call-done = bf16[96,768]{1,0:T(8,128)(2,1)} async-done(((bf16[768,768]{1,0:T(8,128)(2,1)}), bf16[96,768]{1,0:T(8,128)(2,1)}) %reduce-scatter.7.cloned.1.call-update) | async-done | bytes 147472 | tf_op jit(solution)/shard_map/reduce_scatter | solution.py:739
  203.2 52.0 %reduce-scatter.5.cloned.1.call-done = bf16[96,2304]{1,0:T(8,128)(2,1)} async-done(((bf16[768,2304]{1,0:T(8,128)(2,1)}), bf16[96,2304]{1,0:T(8,128)(2,1)}) %reduce-scatter.5.cloned.1.call-update) | async-done | bytes 442384 | tf_op jit(solution)/shard_map/reduce_scatter | solution.py:739
  255.2 57.7 %reduce-scatter.11.cloned.1.call-done = bf16[384,768]{1,0:T(8,128)(2,1)} async-done(((bf16[3072,768]{1,0:T(8,128)(2,1)}), bf16[384,768]{1,0:T(8,128)(2,1)}) %reduce-scatter.11.cloned.1.call-update) | async-done | bytes 589840 | tf_op jit(solution)/shard_map/reduce_scatter | solution.py:739
  312.9 57.2 %reduce-scatter.9.cloned.1.call-done = bf16[96,3072]{1,0:T(8,128)(2,1)} async-done(((bf16[768,3072]{1,0:T(8,128)(2,1)}), bf16[96,3072]{1,0:T(8,128)(2,1)}) %reduce-scatter.9.cloned.1.call-update) | async-done | bytes 589840 | tf_op jit(solution)/shard_map/reduce_scatter | solution.py:739
  370.1 0.0 all-reduce.3.cloned.1.call-update
  370.2 0.0 copy-done.9
  370.2 0.0 copy-done.10
  370.2 42.7 %psum.35 = f32[16,768]{1,0:T(8,128)S(1)} all-reduce(f32[16,768]{1,0:T(8,128)S(1)} %add.53), channel_id=1, replica_groups=mesh['grp'=4,'own'=8] {'grp','own'}, use_global_device_ids=true, to_apply=%region_0.1 | all-reduce | flops 12288 | bytes 98304 | tf_op jit(solution)/shard_map/psum | solution.py:742
  413.0 0.7 dynamic_slice.34
  413.6 0.6 dynamic-slice_bitcast_fusion
  414.2 36.3 %all-reduce.3.cloned.1.call-done = (bf16[96,2304]{1,0:T(8,128)(2,1)}, bf16[96,768]{1,0:T(8,128)(2,1)}, bf16[96,3072]{1,0:T(8,128)(2,1)}, bf16[384,768]{1,0:T(8,128)(2,1)}) async-done(((bf16[96,2304]{1,0:T(8,128)(2,1)}, bf16[96,768]{1,0:T(8,128)(2,1)}, bf16[96,3072]{1,0:T(8,128)(2,1)}, bf16[384,768]{1,0:T(8,128)(2,1)}), (bf16[96,2304]{1,0:T(8,128)(2,1)}, bf16[96,768]{1,0:T(8,128)(2,1)}, ...) | async-done | bytes 1769488 | tf_op jit(solution)/shard_map/psum | solution.py:739
  450.5 2.2 convert_element_type.29
  452.8 2.2 convert_element_type.31
  454.9 0.0 copy-done.7
  454.9 1.0 convert_element_type.25
  455.9 0.0 copy-done.8
  455.9 0.7 convert_element_type.27
  (17 shorter events, 0.1 us)
Async XLA Ops:
  7.2 196.0 %reduce-scatter.7.cloned.1.call-start = ((), (), s32[]{:S(2)}) async-start(), calls=%async_computation.5 | async-start | bytes 1327104 | tf_op jit(solution)/shard_map/reduce_scatter | solution.py:739
  128.8 32.7 %copy-start.2 = (bf16[512,768]{1,0:T(8,128)(2,1)S(1)}, bf16[512,768]{1,0:T(8,128)(2,1)}, u32[]{:S(2)}) copy-start(bf16[512,768]{1,0:T(8,128)(2,1)} %get-tuple-element.66) | copy-start | bytes 2359300
  161.5 2.1 copy-start.5
  161.5 2.1 copy-start.6
  163.6 1.9 copy-start.1
  163.6 2.0 copy-start.4
  165.5 89.7 %reduce-scatter.5.cloned.1.call-start = ((), (), s32[]{:S(2)}) async-start(), calls=%async_computation.4 | async-start | bytes 3981312 | tf_op jit(solution)/shard_map/reduce_scatter | solution.py:739
  165.6 2.0 copy-start.14
  165.6 2.1 copy-start.16
  171.7 1.9 copy-start.12
  171.8 141.1 %reduce-scatter.11.cloned.1.call-start = ((), (), s32[]{:S(2)}) async-start(), calls=%async_computation.7 | async-start | bytes 5308416 | tf_op jit(solution)/shard_map/reduce_scatter | solution.py:739
  173.7 4.0 copy-start.3
  173.7 4.1 copy-start.13
  182.6 1.9 copy-start
  182.6 187.5 %reduce-scatter.9.cloned.1.call-start = ((), (), s32[]{:S(2)}) async-start(), calls=%async_computation.6 | async-start | bytes 5308416 | tf_op jit(solution)/shard_map/reduce_scatter | solution.py:739
  184.5 4.0 copy-start.11
  184.5 4.0 copy-start.15
  193.0 177.1 %copy-start.9 = (f32[16,768]{1,0:T(8,128)S(1)}, f32[16,768]{1,0:T(8,128)}, u32[]{:S(2)}) copy-start(f32[16,768]{1,0:T(8,128)} %get-tuple-element.61) | copy-start | bytes 147460
  193.0 177.1 %copy-start.10 = (f32[16,768]{1,0:T(8,128)S(1)}, f32[16,768]{1,0:T(8,128)}, u32[]{:S(2)}) copy-start(f32[16,768]{1,0:T(8,128)} %get-tuple-element.60) | copy-start | bytes 147460
  193.1 257.5 %all-reduce.3.cloned.1.call-start = ((), (), s32[]{:S(2)}) async-start(), calls=%async_computation.8 | async-start | bytes 3538944 | tf_op jit(solution)/shard_map/psum | solution.py:739
  450.5 4.4 copy-start.7
  450.5 5.4 %copy-start.8 = (bf16[96,768]{1,0:T(8,128)(2,1)S(1)}, bf16[96,768]{1,0:T(8,128)(2,1)}, u32[]{:S(2)}) copy-start(bf16[96,768]{1,0:T(8,128)(2,1)} %get-tuple-element.78) | copy-start | bytes 442372
Sparse Core Ops, SparseCore 0:
  165.6 37.5 reduce-scatter.6
  207.1 48.0 reduce-scatter.4
  259.0 53.8 reduce-scatter.10
  316.2 53.8 reduce-scatter.8
  372.8 77.6 all-reduce.2
